TPU v7x, 512 devices: a whole 4x4x16 slice. The times are simulated.
512 devices in a mesh: slab: 32 (over z_hi, x, core), trace: 16 (over y, z_lo).
Axes of the slice: x: 4, y: 4, z: 16 (z_hi: 4, z_lo: 4; z = z_hi * 4 + z_lo), core: 2. Of those that a mesh axis runs over, the one named last changes fastest.
Arguments:
- transmission: bfloat16 [32, 2048, 2048], P('slab', None, 'trace'), may hold values from -0.125 to 0.125
- reflection: bfloat16 [32, 2048, 2048], P('slab', None, 'trace'), may hold values from -0.0625 to 0.0625
- response: bfloat16 [32, 2048, 2048], P('slab', None, 'trace'), may hold values from -0.125 to 0.125
- sources: bfloat16 [32, 8, 32, 2048], P('slab', None, None, 'trace'), may hold values from -6 to 6
- placement: int32 [8, 32], replicated, may hold values from 0 to 31
Outputs:
- field_trace: bfloat16 [32, 8, 32, 2048], P('slab', None, None, 'trace')
All inputs are finite; a program needn't handle non-finite values.
Results may differ from a plain program's by a relative error of at most 0.018.
Values may be sent and summed in bfloat16 or wider, within the bound.
A program may use at most 64 MiB of HBM per device.

v0:
```python
import jax
import jax.numpy as jnp
from jax import lax
from jax.sharding import Mesh
from jax.sharding import PartitionSpec as P

TRACE = ("trace_0", "trace_1")


def in_order(blocks, dim):
    blocks = jnp.moveaxis(blocks, 0, dim)
    dims = blocks.shape
    return blocks.reshape(*dims[:dim], dims[dim] * dims[dim + 1], *dims[dim + 2 :])


def from_everyone(shard, axis):
    copies = jnp.broadcast_to(shard, (lax.axis_size(axis), *shard.shape))
    return lax.all_to_all(copies, axis, split_axis=0, concat_axis=0, tiled=True)


def gathered_copies(shard, axis, dim):
    return in_order(from_everyone(shard, axis), dim)


def gathered_by_axis(shard, axes, dim):
    if not axes:
        return shard
    nearer = lax.all_gather(shard, axes[-1], axis=dim, tiled=True)
    return gathered_by_axis(nearer, axes[:-1], dim)


def passed_along(shard, axis, by):
    count = lax.axis_size(axis)
    pairs = [(i, i + by) for i in range(count) if 0 <= i + by < count]
    return lax.ppermute(shard, axis, pairs)


def make_adder(matrix, running, portion):
    return running + jnp.dot(portion, matrix, preferred_element_type=jnp.float32)


def run_sweep(driven_units, slab_index, slab_count, crosser):
    unit_count = driven_units.shape[0]
    total_steps = slab_count + unit_count - 1

    def settle(accumulated, tick_now, stored_all):
        active = (tick_now >= 0) & (tick_now < unit_count)
        position = jnp.clip(tick_now, 0, unit_count - 1)
        driven_here = lax.dynamic_index_in_dim(driven_units, position, 0, keepdims=False)
        fresh_trace = (accumulated + driven_here).astype(jnp.bfloat16)
        stored = lax.dynamic_index_in_dim(stored_all, position, 0, keepdims=False)
        chosen = jnp.where(active, fresh_trace, stored)
        stored_all = lax.dynamic_update_index_in_dim(stored_all, chosen, position, 0)
        return (fresh_trace, stored_all)

    def advance(moment, carried):
        carry_down, carry_up, down_all, up_all = carried
        sum_down, sum_up = crosser(carry_down, carry_up)
        tick_down = moment - slab_index
        tick_up = moment - (slab_count - 1 - slab_index)
        carry_down, down_all = settle(sum_down, tick_down, down_all)
        carry_up, up_all = settle(sum_up, tick_up, up_all)
        return (carry_down, carry_up, down_all, up_all)

    start_trace = jnp.zeros(driven_units.shape[1:], jnp.bfloat16)
    start_all = jnp.zeros(driven_units.shape, jnp.bfloat16)
    carried = lax.fori_loop(
        0, total_steps, advance, (start_trace, start_trace, start_all, start_all)
    )
    return (carried[2], carried[3])


def shards(transmission, reflection, response, sources, placement):
    transfer = transmission[0]
    reflect = reflection[0]
    respond = response[0]
    own_sources = sources[0]
    tick_count, batch_count, trace_width = own_sources.shape
    slab_index = lax.axis_index("slab")
    slab_count = lax.axis_size("slab")
    distance = jnp.abs(slab_index - placement).astype(jnp.float32)
    weighting = 1.0 / (1.0 + distance)
    weighted = (own_sources.astype(jnp.float32) * weighting[:, :, None]).astype(jnp.bfloat16)
    total_rows = tick_count * batch_count
    flat_rows = weighted.reshape(total_rows, trace_width)
    empty_rows = jnp.zeros((total_rows, trace_width), jnp.float32)
    driven = make_adder(respond, empty_rows, gathered_copies(flat_rows, TRACE, 1))
    split_count = 1
    whole_transfer = gathered_by_axis(transfer, TRACE, 1)
    own_driven = lax.all_to_all(driven, TRACE, split_axis=0, concat_axis=1, tiled=True)
    rows_here = own_driven.shape[0]
    full_width = own_driven.shape[1]
    driven_units = own_driven.reshape(split_count, rows_here // split_count, full_width)

    def cross_local(carry_down, carry_up):
        from_down = passed_along(carry_down, "slab", 1)
        from_up = passed_along(carry_up, "slab", -1)
        first = jnp.dot(from_down, whole_transfer, preferred_element_type=jnp.float32)
        second = jnp.dot(from_up, whole_transfer, preferred_element_type=jnp.float32)
        return (first, second)

    down_all, up_all = run_sweep(driven_units, slab_index, slab_count, cross_local)
    down_own = down_all.reshape(rows_here, full_width)
    up_own = up_all.reshape(rows_here, full_width)
    down_back, up_back = (
        lax.all_to_all(down_own, TRACE, split_axis=1, concat_axis=0, tiled=True),
        lax.all_to_all(up_own, TRACE, split_axis=1, concat_axis=0, tiled=True),
    )
    down_rows = down_back.astype(jnp.float32)
    up_rows = up_back.astype(jnp.float32)
    contrast = (down_rows - up_rows).astype(jnp.bfloat16)
    combined = make_adder(reflect, down_rows + up_rows, gathered_copies(contrast, TRACE, 1))
    return combined.astype(jnp.bfloat16).reshape(1, tick_count, batch_count, trace_width)


def solution(mesh):
    torus = Mesh(mesh.devices.reshape(mesh.shape["slab"], 4, 4), ("slab", "trace_0", "trace_1"))
    return jax.shard_map(
        shards,
        mesh=torus,
        in_specs=(
            P("slab", None, TRACE),
            P("slab", None, TRACE),
            P("slab", None, TRACE),
            P("slab", None, None, TRACE),
            P(),
        ),
        out_specs=P("slab", None, None, TRACE),
        check_vma=False,
    )
```

profile of v0, /device:TPU:7, one launch (start us, length us, event | category | flops | bytes accessed | tf_op | source)
XLA Modules:
  0.0 829.3 jit_solution(3616945352232155688)
XLA Ops:
  7.3 63.1 %all-gather.5.cloned.1.call-done = bf16[1,2048,512]{2,1,0:T(8,128)(2,1)} async-done(((bf16[1,2048,128]{2,1,0:T(8,128)(2,1)}), bf16[1,2048,512]{2,1,0:T(8,128)(2,1)}) %all-gather.5.cloned.1.call-update) | async-done | bytes 2097168 | tf_op jit(solution)/shard_map/all_gather | solution.py:28
  72.4 31.3 %all_to_all.49 = bf16[16,256,128]{2,1,0:T(8,128)(2,1)S(1)} all-to-all(bf16[16,256,128]{2,1,0:T(8,128)(2,1)S(1)} %broadcast_in_dim.32), channel_id=1, replica_groups=mesh['slab'=32,'trace_0'=4,'trace_1'=4] {'trace_0','trace_1'}, dimensions={0} | all-to-all | bytes 2097152 | tf_op jit(solution)/shard_map/all_to_all | solution.py:18
  109.6 7.4 all-to-all-done.1
  117.1 49.1 %all-gather.7.cloned.1.call-done = bf16[1,2048,2048]{2,1,0:T(8,128)(2,1)} async-done(((bf16[1,2048,512]{2,1,0:T(8,128)(2,1)}), bf16[1,2048,2048]{2,1,0:T(8,128)(2,1)}) %all-gather.7.cloned.1.call-update) | async-done | bytes 8388624 | tf_op jit(solution)/shard_map/all_gather | solution.py:28
  166.2 602.6 %while.21 = (s32[]{:T(128)}, bf16[16,2048]{1,0:T(8,128)(2,1)S(1)}, bf16[16,2048]{1,0:T(8,128)(2,1)S(1)}, bf16[1,16,2048]{2,1,0:T(8,128)(2,1)S(1)}, bf16[1,16,204...) while((s32[]{:T(128)}, bf16[16,2048]{1,0:T(8,128)(2,1)S(1)}, ...), condition=%wide.region_1.2_spmd.clone, body=%wide.region_0.1_spmd.clone.sunk | while | flops 268697600 | bytes 43647296 | solution.py:67
  166.3 7.9 collective-permute-start
  187.0 5.9 collective-permute-start
  205.9 5.9 collective-permute-start
  224.7 5.9 collective-permute-start
  243.4 5.9 collective-permute-start
  318.4 5.9 collective-permute-start
  337.2 5.9 collective-permute-start
  355.9 5.9 collective-permute-start
  431.0 5.9 collective-permute-start
  449.7 5.9 collective-permute-start
  468.5 5.9 collective-permute-start
  487.2 5.9 collective-permute-start
  543.5 5.9 collective-permute-start
  562.3 5.9 collective-permute-start
  581.0 5.9 collective-permute-start
  769.5 8.7 %all-to-all-start.3 = ((bf16[16,16,128]{2,0,1:T(8,128)(2,1)}), bf16[16,16,128]{2,0,1:T(8,128)(2,1)S(1)}, u32[]{:S(2)}, u32[]{:S(2)}) async-start(bf16[16,16,128]{2,0,1:T(8,128)(2,1)} %copy.15), calls=%async_computation.3 | async-start | bytes 131072 | tf_op jit(solution)/shard_map/all_to_all | solution.py:107
  778.2 6.9 all-to-all-done.3
  785.1 9.5 %all_to_all.50 = bf16[16,16,128]{2,0,1:T(8,128)(2,1)S(1)} all-to-all(bf16[16,16,128]{2,0,1:T(8,128)(2,1)S(1)} %copy.14), channel_id=1, replica_groups=mesh['slab'=32,'trace_0'=4,'trace_1'=4] {'trace_0','trace_1'}, dimensions={1} | all-to-all | bytes 131072 | tf_op jit(solution)/shard_map/all_to_all | solution.py:106
  794.9 26.4 %all_to_all.51 = bf16[16,256,128]{1,2,0:T(8,128)(2,1)S(1)} all-to-all(bf16[16,256,128]{1,2,0:T(8,128)(2,1)S(1)} %broadcast_in_dim.33), channel_id=1, replica_groups=mesh['slab'=32,'trace_0'=4,'trace_1'=4] {'trace_0','trace_1'}, dimensions={0} | all-to-all | bytes 2097152 | tf_op jit(solution)/shard_map/all_to_all | solution.py:18
  (495 shorter events, 519.9 us)
Async XLA Ops:
  6.5 63.9 %all-gather.5.cloned.1.call-start = ((), (), s32[]{:S(2)}) async-start(), calls=%async_computation.5 | async-start | bytes 2621440 | tf_op jit(solution)/shard_map/all_gather | solution.py:28
  7.3 158.9 %all-gather.7.cloned.1.call-start = ((), (), s32[]{:S(2)}) async-start(), calls=%async_computation.6 | async-start | bytes 10485760 | tf_op jit(solution)/shard_map/all_gather | solution.py:28
  174.2 11.6 %collective-permute-start.1 = (bf16[16,2048]{1,0:T(8,128)(2,1)S(1)}, bf16[16,2048]{1,0:T(8,128)(2,1)S(1)}, u32[]{:S(2)}, u32[]{:S(2)}) collective-permute-start(bf16[16,2048]{1,0:T(8,128)(2,1)S(1)} %broadcast_select_fusion.5), channel_id=1, source_target_pairs={{16,0},{32,16},{48,32},{64,48},{80,64},{96,80},{112,96},{128,112},... | collective-permute-start | bytes 196616 | tf_op jit(solution)/shard_map/while/body/eval_jaxpr/ppermute | solution.py:35
  193.0 11.6 %collective-permute-start.1 = (bf16[16,2048]{1,0:T(8,128)(2,1)S(1)}, bf16[16,2048]{1,0:T(8,128)(2,1)S(1)}, u32[]{:S(2)}, u32[]{:S(2)}) collective-permute-start(bf16[16,2048]{1,0:T(8,128)(2,1)S(1)} %broadcast_select_fusion.5), channel_id=1, source_target_pairs={{16,0},{32,16},{48,32},{64,48},{80,64},{96,80},{112,96},{128,112},... | collective-permute-start | bytes 196616 | tf_op jit(solution)/shard_map/while/body/eval_jaxpr/ppermute | solution.py:35
  211.8 11.6 %collective-permute-start.1 = (bf16[16,2048]{1,0:T(8,128)(2,1)S(1)}, bf16[16,2048]{1,0:T(8,128)(2,1)S(1)}, u32[]{:S(2)}, u32[]{:S(2)}) collective-permute-start(bf16[16,2048]{1,0:T(8,128)(2,1)S(1)} %broadcast_select_fusion.5), channel_id=1, source_target_pairs={{16,0},{32,16},{48,32},{64,48},{80,64},{96,80},{112,96},{128,112},... | collective-permute-start | bytes 196616 | tf_op jit(solution)/shard_map/while/body/eval_jaxpr/ppermute | solution.py:35
  230.5 11.6 %collective-permute-start.1 = (bf16[16,2048]{1,0:T(8,128)(2,1)S(1)}, bf16[16,2048]{1,0:T(8,128)(2,1)S(1)}, u32[]{:S(2)}, u32[]{:S(2)}) collective-permute-start(bf16[16,2048]{1,0:T(8,128)(2,1)S(1)} %broadcast_select_fusion.5), channel_id=1, source_target_pairs={{16,0},{32,16},{48,32},{64,48},{80,64},{96,80},{112,96},{128,112},... | collective-permute-start | bytes 196616 | tf_op jit(solution)/shard_map/while/body/eval_jaxpr/ppermute | solution.py:35
  249.3 11.6 %collective-permute-start.1 = (bf16[16,2048]{1,0:T(8,128)(2,1)S(1)}, bf16[16,2048]{1,0:T(8,128)(2,1)S(1)}, u32[]{:S(2)}, u32[]{:S(2)}) collective-permute-start(bf16[16,2048]{1,0:T(8,128)(2,1)S(1)} %broadcast_select_fusion.5), channel_id=1, source_target_pairs={{16,0},{32,16},{48,32},{64,48},{80,64},{96,80},{112,96},{128,112},... | collective-permute-start | bytes 196616 | tf_op jit(solution)/shard_map/while/body/eval_jaxpr/ppermute | solution.py:35
  268.1 11.6 %collective-permute-start.1 = (bf16[16,2048]{1,0:T(8,128)(2,1)S(1)}, bf16[16,2048]{1,0:T(8,128)(2,1)S(1)}, u32[]{:S(2)}, u32[]{:S(2)}) collective-permute-start(bf16[16,2048]{1,0:T(8,128)(2,1)S(1)} %broadcast_select_fusion.5), channel_id=1, source_target_pairs={{16,0},{32,16},{48,32},{64,48},{80,64},{96,80},{112,96},{128,112},... | collective-permute-start | bytes 196616 | tf_op jit(solution)/shard_map/while/body/eval_jaxpr/ppermute | solution.py:35
  286.8 11.6 %collective-permute-start.1 = (bf16[16,2048]{1,0:T(8,128)(2,1)S(1)}, bf16[16,2048]{1,0:T(8,128)(2,1)S(1)}, u32[]{:S(2)}, u32[]{:S(2)}) collective-permute-start(bf16[16,2048]{1,0:T(8,128)(2,1)S(1)} %broadcast_select_fusion.5), channel_id=1, source_target_pairs={{16,0},{32,16},{48,32},{64,48},{80,64},{96,80},{112,96},{128,112},... | collective-permute-start | bytes 196616 | tf_op jit(solution)/shard_map/while/body/eval_jaxpr/ppermute | solution.py:35
  305.6 11.6 %collective-permute-start.1 = (bf16[16,2048]{1,0:T(8,128)(2,1)S(1)}, bf16[16,2048]{1,0:T(8,128)(2,1)S(1)}, u32[]{:S(2)}, u32[]{:S(2)}) collective-permute-start(bf16[16,2048]{1,0:T(8,128)(2,1)S(1)} %broadcast_select_fusion.5), channel_id=1, source_target_pairs={{16,0},{32,16},{48,32},{64,48},{80,64},{96,80},{112,96},{128,112},... | collective-permute-start | bytes 196616 | tf_op jit(solution)/shard_map/while/body/eval_jaxpr/ppermute | solution.py:35
  324.3 11.6 %collective-permute-start.1 = (bf16[16,2048]{1,0:T(8,128)(2,1)S(1)}, bf16[16,2048]{1,0:T(8,128)(2,1)S(1)}, u32[]{:S(2)}, u32[]{:S(2)}) collective-permute-start(bf16[16,2048]{1,0:T(8,128)(2,1)S(1)} %broadcast_select_fusion.5), channel_id=1, source_target_pairs={{16,0},{32,16},{48,32},{64,48},{80,64},{96,80},{112,96},{128,112},... | collective-permute-start | bytes 196616 | tf_op jit(solution)/shard_map/while/body/eval_jaxpr/ppermute | solution.py:35
  343.1 11.6 %collective-permute-start.1 = (bf16[16,2048]{1,0:T(8,128)(2,1)S(1)}, bf16[16,2048]{1,0:T(8,128)(2,1)S(1)}, u32[]{:S(2)}, u32[]{:S(2)}) collective-permute-start(bf16[16,2048]{1,0:T(8,128)(2,1)S(1)} %broadcast_select_fusion.5), channel_id=1, source_target_pairs={{16,0},{32,16},{48,32},{64,48},{80,64},{96,80},{112,96},{128,112},... | collective-permute-start | bytes 196616 | tf_op jit(solution)/shard_map/while/body/eval_jaxpr/ppermute | solution.py:35
  361.8 11.6 %collective-permute-start.1 = (bf16[16,2048]{1,0:T(8,128)(2,1)S(1)}, bf16[16,2048]{1,0:T(8,128)(2,1)S(1)}, u32[]{:S(2)}, u32[]{:S(2)}) collective-permute-start(bf16[16,2048]{1,0:T(8,128)(2,1)S(1)} %broadcast_select_fusion.5), channel_id=1, source_target_pairs={{16,0},{32,16},{48,32},{64,48},{80,64},{96,80},{112,96},{128,112},... | collective-permute-start | bytes 196616 | tf_op jit(solution)/shard_map/while/body/eval_jaxpr/ppermute | solution.py:35
  380.6 11.6 %collective-permute-start.1 = (bf16[16,2048]{1,0:T(8,128)(2,1)S(1)}, bf16[16,2048]{1,0:T(8,128)(2,1)S(1)}, u32[]{:S(2)}, u32[]{:S(2)}) collective-permute-start(bf16[16,2048]{1,0:T(8,128)(2,1)S(1)} %broadcast_select_fusion.5), channel_id=1, source_target_pairs={{16,0},{32,16},{48,32},{64,48},{80,64},{96,80},{112,96},{128,112},... | collective-permute-start | bytes 196616 | tf_op jit(solution)/shard_map/while/body/eval_jaxpr/ppermute | solution.py:35
  399.3 11.6 %collective-permute-start.1 = (bf16[16,2048]{1,0:T(8,128)(2,1)S(1)}, bf16[16,2048]{1,0:T(8,128)(2,1)S(1)}, u32[]{:S(2)}, u32[]{:S(2)}) collective-permute-start(bf16[16,2048]{1,0:T(8,128)(2,1)S(1)} %broadcast_select_fusion.5), channel_id=1, source_target_pairs={{16,0},{32,16},{48,32},{64,48},{80,64},{96,80},{112,96},{128,112},... | collective-permute-start | bytes 196616 | tf_op jit(solution)/shard_map/while/body/eval_jaxpr/ppermute | solution.py:35
  418.1 11.6 %collective-permute-start.1 = (bf16[16,2048]{1,0:T(8,128)(2,1)S(1)}, bf16[16,2048]{1,0:T(8,128)(2,1)S(1)}, u32[]{:S(2)}, u32[]{:S(2)}) collective-permute-start(bf16[16,2048]{1,0:T(8,128)(2,1)S(1)} %broadcast_select_fusion.5), channel_id=1, source_target_pairs={{16,0},{32,16},{48,32},{64,48},{80,64},{96,80},{112,96},{128,112},... | collective-permute-start | bytes 196616 | tf_op jit(solution)/shard_map/while/body/eval_jaxpr/ppermute | solution.py:35
  436.9 11.6 %collective-permute-start.1 = (bf16[16,2048]{1,0:T(8,128)(2,1)S(1)}, bf16[16,2048]{1,0:T(8,128)(2,1)S(1)}, u32[]{:S(2)}, u32[]{:S(2)}) collective-permute-start(bf16[16,2048]{1,0:T(8,128)(2,1)S(1)} %broadcast_select_fusion.5), channel_id=1, source_target_pairs={{16,0},{32,16},{48,32},{64,48},{80,64},{96,80},{112,96},{128,112},... | collective-permute-start | bytes 196616 | tf_op jit(solution)/shard_map/while/body/eval_jaxpr/ppermute | solution.py:35
  474.4 11.6 %collective-permute-start.1 = (bf16[16,2048]{1,0:T(8,128)(2,1)S(1)}, bf16[16,2048]{1,0:T(8,128)(2,1)S(1)}, u32[]{:S(2)}, u32[]{:S(2)}) collective-permute-start(bf16[16,2048]{1,0:T(8,128)(2,1)S(1)} %broadcast_select_fusion.5), channel_id=1, source_target_pairs={{16,0},{32,16},{48,32},{64,48},{80,64},{96,80},{112,96},{128,112},... | collective-permute-start | bytes 196616 | tf_op jit(solution)/shard_map/while/body/eval_jaxpr/ppermute | solution.py:35
  493.1 11.6 %collective-permute-start.1 = (bf16[16,2048]{1,0:T(8,128)(2,1)S(1)}, bf16[16,2048]{1,0:T(8,128)(2,1)S(1)}, u32[]{:S(2)}, u32[]{:S(2)}) collective-permute-start(bf16[16,2048]{1,0:T(8,128)(2,1)S(1)} %broadcast_select_fusion.5), channel_id=1, source_target_pairs={{16,0},{32,16},{48,32},{64,48},{80,64},{96,80},{112,96},{128,112},... | collective-permute-start | bytes 196616 | tf_op jit(solution)/shard_map/while/body/eval_jaxpr/ppermute | solution.py:35
  511.9 11.6 %collective-permute-start.1 = (bf16[16,2048]{1,0:T(8,128)(2,1)S(1)}, bf16[16,2048]{1,0:T(8,128)(2,1)S(1)}, u32[]{:S(2)}, u32[]{:S(2)}) collective-permute-start(bf16[16,2048]{1,0:T(8,128)(2,1)S(1)} %broadcast_select_fusion.5), channel_id=1, source_target_pairs={{16,0},{32,16},{48,32},{64,48},{80,64},{96,80},{112,96},{128,112},... | collective-permute-start | bytes 196616 | tf_op jit(solution)/shard_map/while/body/eval_jaxpr/ppermute | solution.py:35
  530.6 11.6 %collective-permute-start.1 = (bf16[16,2048]{1,0:T(8,128)(2,1)S(1)}, bf16[16,2048]{1,0:T(8,128)(2,1)S(1)}, u32[]{:S(2)}, u32[]{:S(2)}) collective-permute-start(bf16[16,2048]{1,0:T(8,128)(2,1)S(1)} %broadcast_select_fusion.5), channel_id=1, source_target_pairs={{16,0},{32,16},{48,32},{64,48},{80,64},{96,80},{112,96},{128,112},... | collective-permute-start | bytes 196616 | tf_op jit(solution)/shard_map/while/body/eval_jaxpr/ppermute | solution.py:35
  549.4 11.6 %collective-permute-start.1 = (bf16[16,2048]{1,0:T(8,128)(2,1)S(1)}, bf16[16,2048]{1,0:T(8,128)(2,1)S(1)}, u32[]{:S(2)}, u32[]{:S(2)}) collective-permute-start(bf16[16,2048]{1,0:T(8,128)(2,1)S(1)} %broadcast_select_fusion.5), channel_id=1, source_target_pairs={{16,0},{32,16},{48,32},{64,48},{80,64},{96,80},{112,96},{128,112},... | collective-permute-start | bytes 196616 | tf_op jit(solution)/shard_map/while/body/eval_jaxpr/ppermute | solution.py:35
  755.7 11.9 %collective-permute-start.1 = (bf16[16,2048]{1,0:T(8,128)(2,1)S(1)}, bf16[16,2048]{1,0:T(8,128)(2,1)S(1)}, u32[]{:S(2)}, u32[]{:S(2)}) collective-permute-start(bf16[16,2048]{1,0:T(8,128)(2,1)S(1)} %broadcast_select_fusion.5), channel_id=1, source_target_pairs={{16,0},{32,16},{48,32},{64,48},{80,64},{96,80},{112,96},{128,112},... | collective-permute-start | bytes 196616 | tf_op jit(solution)/shard_map/while/body/eval_jaxpr/ppermute | solution.py:35
  769.5 15.7 %all-to-all-start.3 = ((bf16[16,16,128]{2,0,1:T(8,128)(2,1)}), bf16[16,16,128]{2,0,1:T(8,128)(2,1)S(1)}, u32[]{:S(2)}, u32[]{:S(2)}) async-start(bf16[16,16,128]{2,0,1:T(8,128)(2,1)} %copy.15), calls=%async_computation.3 | async-start | bytes 131072 | tf_op jit(solution)/shard_map/all_to_all | solution.py:107
  (110 other events, 1763.3 us)
Sparse Core Ops, SparseCore 0:
  9.5 60.9 all-gather.4
  72.5 93.6 all-gather.6
where the time goes:
time: 832 us; the launch traced here: 829 us
  waiting for transfers between devices  283 us (34%)
  starting transfers between devices  263 us (32%)
  matrix products  192 us (23%)
  blocking collectives  67.3 us (8%)
  between operations  13.5 us (2%)
    ppermute x64, starting transfers between devices, passed_along(): return lax.ppermute(shard, axis, pairs)  251 us
    ppermute x64, waiting for transfers between devices, passed_along(): return lax.ppermute(shard, axis, pairs)  156 us
    dot_general x32, matrix products, cross_local(): jnp.dot(from_down, whole_transfer, preferred_element_type=jnp.float32)  151 us
    all_gather x2, waiting for transfers between devices, gathered_by_axis(): nearer = lax.all_gather(shard, axes[-1], axis=dim, tiled=True)  112 us
    all_to_all x2, blocking collectives, from_everyone(): return lax.all_to_all(copies, axis, split_axis=0, concat_axis=0, tiled=True)  57.8 us
    dot_general x32, matrix products, cross_local(): jnp.dot(from_up, whole_transfer, preferred_element_type=jnp.float32)  38.4 us
  transfers between devices with their start and end apart: 68, of which 36 were waited for; matrix products, arithmetic and copies ran while one was open for 19% of the time, Pallas kernels for 0%

commit v1 on v0

v1 whole, which is shorter than its diff:
```python
import functools

import jax
import jax.numpy as jnp
from jax import lax
from jax.experimental import pallas as pl
from jax.experimental.pallas import tpu as pltpu
from jax.sharding import Mesh
from jax.sharding import PartitionSpec as P

TRACE = ("trace_0", "trace_1")
MESH = pl.DeviceIdType.MESH
CHUNKS = 4
FUSE_FROM = 4


def dot(a, b):
    return jnp.dot(a, b, preferred_element_type=jnp.float32)


def chain_kernel(
    slabs,
    t_ref,
    drv_ref,
    contrast_ref,
    total_ref,
    t_own,
    t_oth,
    fused,
    drv_oth,
    local,
    x_in,
    z_out,
    z_in,
    y_own,
    load_sem,
    t_send,
    t_recv,
    d_send,
    d_recv,
    x_send,
    x_recv,
    z_send,
    z_recv,
):
    slab = lax.axis_index("slab")
    row = lax.axis_index("trace_0")
    col = lax.axis_index("trace_1")
    core = slab % 2
    chip = slab // 2
    last = slabs // 2 - 1
    place = chip * (1 - 2 * core) + last * core
    partner = (slab + 1 - 2 * core, row, col)
    following = ((slab + 2 - 4 * core + slabs) % slabs, row, col)
    previous = ((slab - 2 + 4 * core + slabs) % slabs, row, col)
    width = t_own.shape[0]
    step = width // CHUNKS

    barrier = pltpu.get_barrier_semaphore()
    for device in (partner, following, previous):
        pl.semaphore_signal(barrier, inc=1, device_id=device, device_id_type=MESH)
    pl.semaphore_wait(barrier, 3)

    give_t = pltpu.make_async_remote_copy(
        src_ref=t_ref, dst_ref=t_oth, send_sem=t_send, recv_sem=t_recv, device_id=partner, device_id_type=MESH
    )
    give_t.start()
    give_d = pltpu.make_async_remote_copy(
        src_ref=drv_ref, dst_ref=drv_oth, send_sem=d_send, recv_sem=d_recv, device_id=partner, device_id_type=MESH
    )
    give_d.start()
    load = pltpu.make_async_copy(t_ref, t_own, load_sem)
    load.start()
    load.wait()
    give_d.wait()
    give_t.wait()

    def columns(j):
        return pl.ds(j * step, step)

    def onward(j):
        return pltpu.make_async_remote_copy(
            src_ref=z_out.at[:, columns(j)],
            dst_ref=x_in.at[:, columns(j)],
            send_sem=x_send.at[j],
            recv_sem=x_recv.at[j],
            device_id=following,
            device_id_type=MESH,
        )

    def emit(j, value):
        z_out[:, columns(j)] = value.astype(jnp.bfloat16)

        @pl.when(place < last)
        def _():
            onward(j).start()

    @pl.when(place == 0)
    def _():
        y_own[...] = drv_ref[...].astype(jnp.bfloat16)
        for j in range(CHUNKS):
            emit(j, dot(y_own[...], t_oth[:, columns(j)]) + drv_oth[:, columns(j)])

    @pl.when((place > 0) & (place < FUSE_FROM))
    def _():
        for j in range(CHUNKS):
            onward(j).wait_recv()
        for j in range(CHUNKS):
            here = dot(x_in[...], t_own[:, columns(j)]) + drv_ref[:, columns(j)]
            y_own[:, columns(j)] = here.astype(jnp.bfloat16)
        for j in range(CHUNKS):
            emit(j, dot(y_own[...], t_oth[:, columns(j)]) + drv_oth[:, columns(j)])

    @pl.when(place >= FUSE_FROM)
    def _():
        local[...] = dot(drv_ref[...].astype(jnp.bfloat16), t_oth[...]) + drv_oth[...]
        tall, wide = width // 4, width // 8

        def block(i, carry):
            rows = pl.ds(pl.multiple_of((i % 4) * tall, tall), tall)
            cols = pl.ds(pl.multiple_of((i // 4) * wide, wide), wide)
            fused[rows, cols] = dot(t_own[rows, :], t_oth[:, cols]).astype(jnp.bfloat16)
            return carry

        lax.fori_loop(0, 32, block, 0)
        for j in range(CHUNKS):
            onward(j).wait_recv()
        for j in range(CHUNKS):
            emit(j, dot(x_in[...], fused[:, columns(j)]) + local[:, columns(j)])
        for j in range(CHUNKS):
            here = dot(x_in[...], t_own[:, columns(j)]) + drv_ref[:, columns(j)]
            y_own[:, columns(j)] = here.astype(jnp.bfloat16)

    swap = pltpu.make_async_remote_copy(
        src_ref=z_out, dst_ref=z_in, send_sem=z_send, recv_sem=z_recv, device_id=partner, device_id_type=MESH
    )
    swap.start()
    swap.wait()
    mine = y_own[...].astype(jnp.float32)
    other = z_in[...].astype(jnp.float32)
    sign = (1 - 2 * core).astype(jnp.float32)
    contrast_ref[...] = ((mine - other) * sign).astype(jnp.bfloat16)
    total_ref[...] = (mine + other).astype(jnp.bfloat16)

    @pl.when(place < last)
    def _():
        for j in range(CHUNKS):
            onward(j).wait_send()


def run_chain(transfer, driven, slabs):
    rows, width = driven.shape
    vmem = pl.BlockSpec(memory_space=pltpu.VMEM)
    dma = pltpu.SemaphoreType.DMA
    trace = jax.ShapeDtypeStruct((rows, width), jnp.bfloat16)
    operator = pltpu.VMEM((width, width), jnp.bfloat16)
    narrow = pltpu.VMEM((rows, width), jnp.bfloat16)
    full = pltpu.VMEM((rows, width), jnp.float32)
    return pl.pallas_call(
        functools.partial(chain_kernel, slabs),
        out_shape=(trace, trace),
        in_specs=[pl.BlockSpec(memory_space=pl.ANY), vmem],
        out_specs=(vmem, vmem),
        scratch_shapes=[operator, operator, operator, full, full, narrow, narrow, narrow, narrow]
        + [dma] * 5
        + [dma((CHUNKS,))] * 2
        + [dma] * 2,
        compiler_params=pltpu.CompilerParams(
            collective_id=0, has_side_effects=True, vmem_limit_bytes=48 * 2**20
        ),
        name="chain",
    )(transfer, driven)


def shards(slabs, transmission, reflection, response, sources, placement):
    transfer = transmission[0]
    reflect = reflection[0]
    respond = response[0]
    own_sources = sources[0]
    ticks, batch, depth = own_sources.shape
    rows = ticks * batch
    slab = lax.axis_index("slab")
    distance = jnp.abs(slab - placement).astype(jnp.float32)
    weighting = 1.0 / (1.0 + distance)
    weighted = (own_sources.astype(jnp.float32) * weighting[:, :, None]).astype(jnp.bfloat16)
    flat = weighted.reshape(rows, depth)
    every = lax.all_gather(flat, TRACE, axis=1, tiled=True)
    driven = dot(every, respond)
    nearer = lax.all_gather(transfer, "trace_1", axis=1, tiled=True)
    whole = lax.all_gather(nearer, "trace_0", axis=1, tiled=True)
    own_driven = lax.all_to_all(driven, TRACE, split_axis=0, concat_axis=1, tiled=True)
    contrast, total = run_chain(whole, own_driven, slabs)
    contrast = lax.all_gather(contrast, TRACE, axis=0, tiled=True)
    total = lax.all_to_all(total, TRACE, split_axis=1, concat_axis=0, tiled=True)
    combined = total.astype(jnp.float32) + dot(contrast, reflect)
    return combined.astype(jnp.bfloat16).reshape(1, ticks, batch, depth)


def solution(mesh):
    slabs = mesh.shape["slab"]
    torus = Mesh(mesh.devices.reshape(slabs, 4, 4), ("slab",) + TRACE)
    return jax.shard_map(
        functools.partial(shards, slabs),
        mesh=torus,
        in_specs=(
            P("slab", None, TRACE),
            P("slab", None, TRACE),
            P("slab", None, TRACE),
            P("slab", None, None, TRACE),
            P(),
        ),
        out_specs=P("slab", None, None, TRACE),
        check_vma=False,
    )
```

time: 832 us -> 431 us (0.52)
  the two profiles are of different devices: /device:TPU:7 before, /device:TPU:24 now
where the time goes in v1:
time: 431 us; the launch traced here: 425 us
  waiting for transfers between devices  283 us (66%)
  Pallas kernels  96.7 us (22%)
  blocking collectives  25.6 us (6%)
  between operations  13.2 us (3%)
    pallas_call x1, Pallas kernels, run_chain(): pl.pallas_call(functools.partial(chain_kernel, slabs), out_shape=(trace,...  96.7 us
    all_gather x1, waiting for transfers between devices, shards(): every = lax.all_gather(flat, TRACE, axis=1, tiled=True)  76.2 us
    all_gather x1, waiting for transfers between devices, shards(): whole = lax.all_gather(nearer, 'trace_0', axis=1, tiled=True)  74.9 us
    all_gather x1, waiting for transfers between devices, shards(): contrast = lax.all_gather(contrast, TRACE, axis=0, tiled=True)  70.3 us
    all_gather x1, waiting for transfers between devices, shards(): nearer = lax.all_gather(transfer, 'trace_1', axis=1, tiled=True)  60.4 us
    all_to_all x1, blocking collectives, shards(): lax.all_to_all(driven, TRACE, split_axis=0, concat_axis=1, tiled=True)  14.2 us
    all_to_all x1, blocking collectives, shards(): lax.all_to_all(total, TRACE, split_axis=1, concat_axis=0, tiled=True)  11.4 us
  transfers between devices with their start and end apart: 4, of which 4 were waited for; matrix products, arithmetic and copies ran while one was open for 1% of the time, Pallas kernels for 0%

profile of v1, /device:TPU:24, one launch (start us, length us, event | category | flops | bytes accessed | tf_op | source)
XLA Modules:
  0.0 424.6 jit_solution(4665763457413150325)
XLA Ops:
  6.5 0.0 copy-start
  6.5 0.0 copy-start.1
  6.5 0.0 all-gather.11.cloned.1.call-start
  6.5 0.7 all-gather.11.cloned.1.call-update
  7.3 0.0 all-gather.7.cloned.1.call-start
  7.3 0.7 add_divide_fusion
  8.0 0.1 mul.11
  8.1 1.6 fusion.4
  9.7 0.0 all-gather.7.cloned.1.call-update
  9.7 0.0 all-gather.13.cloned.1.call-start
  9.7 60.4 %all-gather.11.cloned.1.call-done = bf16[1,2048,512]{2,1,0:T(8,128)(2,1)} async-done(((bf16[1,2048,128]{2,1,0:T(8,128)(2,1)}), bf16[1,2048,512]{2,1,0:T(8,128)(2,1)}) %all-gather.11.cloned.1.call-update) | async-done | bytes 2097168 | tf_op jit(solution)/shard_map/all_gather | solution.py:189
  70.1 0.0 all-gather.13.cloned.1.call-update
  70.1 0.0 all-gather.9.cloned.1.call-start
  70.2 76.2 %all-gather.7.cloned.1.call-done = bf16[256,2048]{1,0:T(8,128)(2,1)} async-done(((bf16[256,128]{1,0:T(8,128)(2,1)}), bf16[256,2048]{1,0:T(8,128)(2,1)}) %all-gather.7.cloned.1.call-update) | async-done | bytes 1048592 | tf_op jit(solution)/shard_map/all_gather | solution.py:187
  146.4 0.0 copy-done
  146.4 1.6 fusion.2
  148.0 14.2 %all_to_all.29 = f32[16,16,128]{2,1,0:T(8,128)S(1)} all-to-all(f32[16,16,128]{2,1,0:T(8,128)S(1)} %fusion.2), channel_id=1, replica_groups=mesh['slab'=32,'trace_0'=4,'trace_1'=4] {'trace_0','trace_1'}, dimensions={0} | all-to-all | bytes 262144 | tf_op jit(solution)/shard_map/all_to_all | solution.py:191
  162.3 74.9 %all-gather.13.cloned.1.call-done = bf16[1,2048,2048]{2,1,0:T(8,128)(2,1)} async-done(((bf16[1,2048,512]{2,1,0:T(8,128)(2,1)}), bf16[1,2048,2048]{2,1,0:T(8,128)(2,1)}) %all-gather.13.cloned.1.call-update) | async-done | bytes 8388624 | tf_op jit(solution)/shard_map/all_gather | solution.py:190
  237.2 96.7 %chain.1 = (bf16[16,2048]{1,0:T(8,128)(2,1)}, bf16[16,2048]{1,0:T(8,128)(2,1)S(1)}) custom-call(bf16[2048,2048]{1,0:T(8,128)(2,1)} %bitcast.29, f32[16,2048]{1,0:T(8,128)S(1)} %copy_bitcast_fusion.drv_ref), custom_call_target="tpu_custom_call" | custom-call | tf_op jit(solution)/shard_map/chain/pallas_call | solution.py:159
  334.0 0.0 all-gather.9.cloned.1.call-update
  334.0 11.4 %all_to_all.30 = bf16[16,16,128]{2,0,1:T(8,128)(2,1)S(1)} all-to-all(bf16[16,16,128]{2,0,1:T(8,128)(2,1)S(1)} %copy_bitcast_fusion.1), channel_id=1, replica_groups=mesh['slab'=32,'trace_0'=4,'trace_1'=4] {'trace_0','trace_1'}, dimensions={1} | all-to-all | bytes 131072 | tf_op jit(solution)/shard_map/all_to_all | solution.py:194
  345.4 70.3 %all-gather.9.cloned.1.call-done = bf16[256,2048]{1,0:T(8,128)(2,1)} async-done(((bf16[16,2048]{1,0:T(8,128)(2,1)}), bf16[256,2048]{1,0:T(8,128)(2,1)}) %all-gather.9.cloned.1.call-update) | async-done | bytes 1048592 | tf_op jit(solution)/shard_map/all_gather | solution.py:193
  415.8 0.0 copy-done.1
  415.8 2.3 fusion
  (3 shorter events, 0.0 us)
Async XLA Ops:
  6.5 139.9 %copy-start = (bf16[1,2048,128]{2,1,0:T(8,128)(2,1)S(1)}, bf16[1,2048,128]{2,1,0:T(8,128)(2,1)}, u32[]{:S(2)}) copy-start(bf16[1,2048,128]{2,1,0:T(8,128)(2,1)} %param.7) | copy-start | bytes 1572868
  6.5 409.2 %copy-start.1 = (bf16[1,2048,128]{2,1,0:T(8,128)(2,1)S(1)}, bf16[1,2048,128]{2,1,0:T(8,128)(2,1)}, u32[]{:S(2)}) copy-start(bf16[1,2048,128]{2,1,0:T(8,128)(2,1)} %param.6) | copy-start | bytes 1572868
  6.5 63.6 %all-gather.11.cloned.1.call-start = ((), (), s32[]{:S(2)}) async-start(), calls=%async_computation.4 | async-start | bytes 2621440 | tf_op jit(solution)/shard_map/all_gather | solution.py:189
  7.3 139.1 %all-gather.7.cloned.1.call-start = ((), (), s32[]{:S(2)}) async-start(), calls=%async_computation.2 | async-start | bytes 1114112 | tf_op jit(solution)/shard_map/all_gather | solution.py:187
  9.7 227.5 %all-gather.13.cloned.1.call-start = ((), (), s32[]{:S(2)}) async-start(), calls=%async_computation.5 | async-start | bytes 10485760 | tf_op jit(solution)/shard_map/all_gather | solution.py:190
  70.1 345.6 %all-gather.9.cloned.1.call-start = ((), (), s32[]{:S(2)}) async-start(), calls=%async_computation.3 | async-start | bytes 1114112 | tf_op jit(solution)/shard_map/all_gather | solution.py:193
Sparse Core Ops, SparseCore 0:
  9.5 60.6 all-gather.10
  72.1 74.2 all-gather.6
  148.5 88.6 all-gather.12
  334.1 81.6 all-gather.8

commit v2 on v1

v2 whole, which is shorter than its diff:
```python
import functools

import jax
import jax.numpy as jnp
from jax import lax
from jax.experimental import pallas as pl
from jax.experimental.pallas import tpu as pltpu
from jax.sharding import Mesh
from jax.sharding import PartitionSpec as P

TRACE = ("trace_0", "trace_1")
MESH = pl.DeviceIdType.MESH
SIDE = 4
CHUNKS = 4
FUSE_FROM = 6
bf16 = jnp.bfloat16
f32 = jnp.float32


def dot(a, b):
    return jnp.dot(a, b, preferred_element_type=f32)


def loop(count, body):
    def step(i, carry):
        body(i)
        return carry

    lax.fori_loop(0, count, step, 0)


class Spread:
    def __init__(self, place, own, view, sems, extra=None):
        self.slab, self.row, self.col = place
        self.own, self.view, self.extra = own, view, extra
        self.arrived, self.up, self.down, self.fore, self.back = sems

    def copies(self, source, block, half, up, down, fore, back, run):
        row, col = self.row, self.col

        def send(sem, device):
            run(
                pltpu.make_async_remote_copy(
                    src_ref=source,
                    dst_ref=self.view(block, half),
                    send_sem=sem.at[block, half],
                    recv_sem=self.arrived.at[block, half],
                    device_id=device,
                    device_id_type=MESH,
                )
            )

        @pl.when(up)
        def _():
            send(self.up, (self.slab, row, jnp.minimum(col + 1, SIDE - 1)))

        @pl.when(down)
        def _():
            send(self.down, (self.slab, row, jnp.maximum(col - 1, 0)))

        @pl.when(fore)
        def _():
            send(self.fore, (self.slab, (row + 1) % SIDE, col))

        @pl.when(back)
        def _():
            send(self.back, (self.slab, (row + SIDE - 1) % SIDE, col))

        if self.extra is not None:
            run(self.extra(source, block, half))

    def await_piece(self, block, half):
        piece = self.view(block, half)
        pltpu.make_async_copy(piece, piece, self.arrived.at[block, half]).wait()

    def first(self, run):
        yes = self.row >= 0
        block = self.row * SIDE + self.col

        def piece(half):
            self.copies(self.own(half), block, half, self.col < SIDE - 1, self.col > 0, yes, yes, run)

        loop(2, piece)

    def rest(self, run, receive):
        row, col = self.row, self.col
        yes, no = row >= 0, row < 0

        def pieces(distance, body):
            def one(i):
                side = 2 * (i // 2) - 1
                at = col + side * distance
                there = (at >= 0) & (at < SIDE) & (distance >= 0) & ((distance > 0) | (side < 0))

                @pl.when(there)
                def _():
                    body(side, at, i % 2)

            loop(4, one)

        def handle(block, half, up, down, fore, back):
            if receive:
                self.await_piece(block, half)
            self.copies(self.view(block, half), block, half, up, down, fore, back, run)

        def along(side, at, half):
            up = (side < 0) & (col < SIDE - 1)
            down = (side > 0) & (col > 0)
            handle(row * SIDE + at, half, up, down, yes, yes)

        def around(side, at, half):
            handle((row + SIDE - 1) % SIDE * SIDE + at, half, no, no, half == 0, no)
            handle((row + 1) % SIDE * SIDE + at, half, no, no, no, half == 1)

        def across(side, at, half):
            handle((row + 2) % SIDE * SIDE + at, half, no, no, no, no)

        def turn(r):
            @pl.when(r < SIDE - 1)
            def _():
                pieces(r + 1, along)

            pieces(r, around)
            pieces(r - 1, across)

        loop(SIDE + 1, turn)


def start(copy):
    copy.start()


def wait_send(copy):
    copy.wait_send()


def sweep_kernel(
    slabs,
    transfer_ref,
    respond_ref,
    reflect_ref,
    weighted_ref,
    out_ref,
    t_own,
    t_oth,
    fused,
    respond,
    reflect,
    sources,
    driven,
    drv_own,
    drv_oth,
    local,
    x_in,
    z_out,
    z_in,
    y_own,
    contrast,
    total,
    totals,
    load_sem,
    d_send,
    d_recv,
    x_send,
    x_recv,
    z_send,
    z_recv,
    exchange_send,
    exchange_recv,
    core_send,
    core_recv,
    *spread_sems,
):
    slab = lax.axis_index("slab")
    row = lax.axis_index("trace_0")
    col = lax.axis_index("trace_1")
    trace = row * SIDE + col
    peers = SIDE * SIDE
    core = slab % 2
    chip = slab // 2
    last = slabs // 2 - 1
    place = chip * (1 - 2 * core) + last * core
    partner = (slab + 1 - 2 * core, row, col)
    following = ((slab + 2 - 4 * core + slabs) % slabs, row, col)
    previous = ((slab - 2 + 4 * core + slabs) % slabs, row, col)
    width = t_own.shape[0]
    depth = respond.shape[1]
    rows = sources.shape[0]
    share = rows // peers
    step = width // CHUNKS

    def peer(j):
        other = (trace + 1 + j) % peers
        return other, (slab, other // SIDE, other % SIDE)

    barrier = pltpu.get_barrier_semaphore()

    def greet(j):
        pl.semaphore_signal(barrier, inc=1, device_id=peer(j)[1], device_id_type=MESH)

    for device in (partner, following, previous):
        pl.semaphore_signal(barrier, inc=1, device_id=device, device_id_type=MESH)
    loop(peers - 1, greet)

    def block_columns(b):
        return pl.ds(pl.multiple_of(b * depth, depth), depth)

    def block_rows(b):
        return pl.ds(pl.multiple_of(b * share, share), share)

    loads = [
        pltpu.make_async_copy(transfer_ref, t_own.at[:, block_columns(trace)], load_sem.at[0]),
        pltpu.make_async_copy(weighted_ref, sources.at[:, block_columns(trace)], load_sem.at[1]),
        pltpu.make_async_copy(respond_ref, respond, load_sem.at[2]),
        pltpu.make_async_copy(reflect_ref, reflect, load_sem.at[3]),
    ]
    for load in loads:
        load.start()
    pl.semaphore_wait(barrier, peers + 2)

    def half_rows(count, half):
        return pl.ds(pl.multiple_of(half * (count // 2), count // 2), count // 2)

    here = (slab, row, col)

    def to_partner(source, block, half):
        return pltpu.make_async_remote_copy(
            src_ref=source,
            dst_ref=t_oth.at[half_rows(width, half), block_columns(block)],
            send_sem=core_send.at[block, half],
            recv_sem=core_recv.at[block, half],
            device_id=partner,
            device_id_type=MESH,
        )

    source_spread = Spread(
        here,
        lambda half: weighted_ref.at[half_rows(rows, half), :],
        lambda block, half: sources.at[half_rows(rows, half), block_columns(block)],
        spread_sems[0:5],
    )
    transfer_spread = Spread(
        here,
        lambda half: transfer_ref.at[half_rows(width, half), :],
        lambda block, half: t_own.at[half_rows(width, half), block_columns(block)],
        spread_sems[5:10],
        to_partner,
    )
    contrast_spread = Spread(
        here,
        lambda half: contrast.at[block_rows(trace), half_rows(width, half)],
        lambda block, half: contrast.at[block_rows(block), half_rows(width, half)],
        spread_sems[10:15],
    )

    source_spread.first(start)
    transfer_spread.first(start)
    source_spread.rest(start, True)
    for load in loads:
        load.wait()

    driven[...] = dot(sources[...], respond[...])

    def give_driven(j):
        other, device = peer(j)
        return pltpu.make_async_remote_copy(
            src_ref=driven.at[block_rows(other), :],
            dst_ref=drv_own.at[:, block_columns(trace)],
            send_sem=exchange_send.at[0, other],
            recv_sem=exchange_recv.at[0, trace],
            device_id=device,
            device_id_type=MESH,
        )

    loop(peers - 1, lambda j: give_driven(j).start())
    drv_own[:, block_columns(trace)] = driven[block_rows(trace), :]

    transfer_spread.rest(start, True)

    def take_driven(j):
        other, _ = peer(j)
        piece = drv_own.at[:, block_columns(other)]
        pltpu.make_async_copy(piece, piece, exchange_recv.at[0, other]).wait()

    loop(peers - 1, take_driven)
    give_d = pltpu.make_async_remote_copy(
        src_ref=drv_own, dst_ref=drv_oth, send_sem=d_send, recv_sem=d_recv, device_id=partner, device_id_type=MESH
    )
    give_d.start()

    def take_transfer(i):
        piece = t_oth.at[half_rows(width, i % 2), block_columns(i // 2)]
        pltpu.make_async_copy(piece, piece, core_recv.at[i // 2, i % 2]).wait()

    loop(2 * peers, take_transfer)
    give_d.wait()

    def columns(j):
        return pl.ds(j * step, step)

    def onward(j):
        return pltpu.make_async_remote_copy(
            src_ref=z_out.at[:, columns(j)],
            dst_ref=x_in.at[:, columns(j)],
            send_sem=x_send.at[j],
            recv_sem=x_recv.at[j],
            device_id=following,
            device_id_type=MESH,
        )

    def emit(j, value):
        z_out[:, columns(j)] = value.astype(bf16)

        @pl.when(place < last)
        def _():
            onward(j).start()

    @pl.when(place == 0)
    def _():
        y_own[...] = drv_own[...].astype(bf16)
        for j in range(CHUNKS):
            emit(j, dot(y_own[...], t_oth[:, columns(j)]) + drv_oth[:, columns(j)])

    @pl.when((place > 0) & (place < FUSE_FROM))
    def _():
        for j in range(CHUNKS):
            onward(j).wait_recv()
        for j in range(CHUNKS):
            value = dot(x_in[...], t_own[:, columns(j)]) + drv_own[:, columns(j)]
            y_own[:, columns(j)] = value.astype(bf16)
        for j in range(CHUNKS):
            emit(j, dot(y_own[...], t_oth[:, columns(j)]) + drv_oth[:, columns(j)])

    @pl.when(place >= FUSE_FROM)
    def _():
        local[...] = dot(drv_own[...].astype(bf16), t_oth[...]) + drv_oth[...]
        tall, wide = width // 4, width // 8

        def block(i):
            at = pl.ds(pl.multiple_of((i % 4) * tall, tall), tall)
            to = pl.ds(pl.multiple_of((i // 4) * wide, wide), wide)
            fused[at, to] = dot(t_own[at, :], t_oth[:, to]).astype(bf16)

        loop(32, block)
        for j in range(CHUNKS):
            onward(j).wait_recv()
        for j in range(CHUNKS):
            emit(j, dot(x_in[...], fused[:, columns(j)]) + local[:, columns(j)])
        for j in range(CHUNKS):
            value = dot(x_in[...], t_own[:, columns(j)]) + drv_own[:, columns(j)]
            y_own[:, columns(j)] = value.astype(bf16)

    swap = pltpu.make_async_remote_copy(
        src_ref=z_out, dst_ref=z_in, send_sem=z_send, recv_sem=z_recv, device_id=partner, device_id_type=MESH
    )
    swap.start()
    swap.wait()
    mine = y_own[...].astype(f32)
    other_way = z_in[...].astype(f32)
    sign = (1 - 2 * core).astype(f32)
    contrast[block_rows(trace), :] = ((mine - other_way) * sign).astype(bf16)
    total[...] = mine + other_way
    contrast_spread.first(start)

    def give_total(j):
        other, device = peer(j)
        return pltpu.make_async_remote_copy(
            src_ref=total.at[:, block_columns(other)],
            dst_ref=totals.at[block_rows(trace), :],
            send_sem=exchange_send.at[1, other],
            recv_sem=exchange_recv.at[1, trace],
            device_id=device,
            device_id_type=MESH,
        )

    loop(peers - 1, lambda j: give_total(j).start())
    totals[block_rows(trace), :] = total[:, block_columns(trace)]
    contrast_spread.rest(start, True)

    def take_total(j):
        other, _ = peer(j)
        piece = totals.at[block_rows(other), :]
        pltpu.make_async_copy(piece, piece, exchange_recv.at[1, other]).wait()

    loop(peers - 1, take_total)
    out_ref[...] = (totals[...] + dot(contrast[...], reflect[...])).astype(bf16)

    @pl.when(place < last)
    def _():
        for j in range(CHUNKS):
            onward(j).wait_send()

    loop(peers - 1, lambda j: give_driven(j).wait_send())
    loop(peers - 1, lambda j: give_total(j).wait_send())
    for spread in (source_spread, transfer_spread, contrast_spread):
        spread.first(wait_send)
        spread.rest(wait_send, False)


def sweep(transfer, respond, reflect, weighted, slabs):
    width, depth = transfer.shape
    rows = weighted.shape[0]
    peers = SIDE * SIDE
    share = rows // peers
    anywhere = pl.BlockSpec(memory_space=pl.ANY)
    vmem = pl.BlockSpec(memory_space=pltpu.VMEM)
    dma = pltpu.SemaphoreType.DMA
    operator = pltpu.VMEM((width, width), bf16)
    narrow = pltpu.VMEM((share, width), bf16)
    full = pltpu.VMEM((share, width), f32)
    return pl.pallas_call(
        functools.partial(sweep_kernel, slabs),
        out_shape=jax.ShapeDtypeStruct((rows, depth), bf16),
        in_specs=[anywhere] * 4,
        out_specs=vmem,
        scratch_shapes=[
            operator,
            operator,
            operator,
            pltpu.VMEM((width, depth), bf16),
            pltpu.VMEM((width, depth), bf16),
            pltpu.VMEM((rows, width), bf16),
            pltpu.VMEM((rows, depth), f32),
            full,
            full,
            full,
            narrow,
            narrow,
            narrow,
            narrow,
            pltpu.VMEM((rows, width), bf16),
            full,
            pltpu.VMEM((rows, depth), f32),
            dma((4,)),
            dma,
            dma,
            dma((CHUNKS,)),
            dma((CHUNKS,)),
            dma,
            dma,
            dma((2, peers)),
            dma((2, peers)),
            dma((peers, 2)),
            dma((peers, 2)),
        ]
        + [dma((peers, 2))] * 15,
        compiler_params=pltpu.CompilerParams(
            collective_id=0, has_side_effects=True, vmem_limit_bytes=44 * 2**20
        ),
        name="sweep",
    )(transfer, respond, reflect, weighted)


def shards(slabs, transmission, reflection, response, sources, placement):
    own_sources = sources[0]
    ticks, batch, depth = own_sources.shape
    rows = ticks * batch
    slab = lax.axis_index("slab")
    distance = jnp.abs(slab - placement).astype(f32)
    weighting = 1.0 / (1.0 + distance)
    weighted = (own_sources.astype(f32) * weighting[:, :, None]).astype(bf16)
    combined = sweep(
        transmission[0], response[0], reflection[0], weighted.reshape(rows, depth), slabs
    )
    return combined.reshape(1, ticks, batch, depth)


def solution(mesh):
    slabs = mesh.shape["slab"]
    torus = Mesh(mesh.devices.reshape(slabs, SIDE, SIDE), ("slab",) + TRACE)
    return jax.shard_map(
        functools.partial(shards, slabs),
        mesh=torus,
        in_specs=(
            P("slab", None, TRACE),
            P("slab", None, TRACE),
            P("slab", None, TRACE),
            P("slab", None, None, TRACE),
            P(),
        ),
        out_specs=P("slab", None, None, TRACE),
        check_vma=False,
    )
```

time: 431 us -> 207 us (0.48)
  the two profiles are of different devices: /device:TPU:24 before, /device:TPU:486 now
where the time goes in v2:
time: 207 us; the launch traced here: 206 us
  Pallas kernels  201 us (97%)
  local copies, waits for them, and re-layouts  4.52 us (2%)
    pallas_call x1, Pallas kernels, sweep(): pl.pallas_call(functools.partial(sweep_kernel, slabs), out_shape=jax.Shap...  201 us
    unnamed x9, local copies, waits for them, and re-layouts  4.44 us

profile of v2, /device:TPU:486, one launch (start us, length us, event | category | flops | bytes accessed | tf_op | source)
XLA Modules:
  0.0 206.5 jit_solution(4146953548731492347)
XLA Ops:
  0.0 0.0 copy-start.3
  0.0 0.7 copy-done.3
  0.7 0.1 mul.11
  0.8 0.9 fusion.weighted_ref
  1.7 0.0 copy-start
  1.7 1.0 copy-done
  2.8 0.0 copy-start.1
  2.8 1.0 copy-done.1
  3.8 0.0 copy-start.2
  3.8 1.0 copy-done.2
  4.9 201.0 %sweep.1 = bf16[256,128]{1,0:T(8,128)(2,1)S(1)} custom-call(bf16[2048,128]{1,0:T(8,128)(2,1)S(1)} %bitcast.7, bf16[2048,128]{1,0:T(8,128)(2,1)S(1)} %bitcast.8, bf16[2048,128]{1,0:T(8,128)(2,1)S(1)} %bitcast.9, bf16[256,128]{1,0:T(8,128)(2,1)S(1)} %fusion.weighted_ref), custom_call_target="tpu_custom_call" | custom-call | tf_op jit(solution)/shard_map/sweep/pallas_call | solution.py:411
  205.8 0.6 copy.7
  (1 shorter events, 0.0 us)
Async XLA Ops:
  0.0 0.7 copy-start.3
  1.7 1.0 copy-start
  2.8 1.0 copy-start.1
  3.8 1.0 copy-start.2

commit v3 on v2

--- a/solution.py
+++ b/solution.py
@@ -12,7 +12,9 @@
 MESH = pl.DeviceIdType.MESH
 SIDE = 4
 CHUNKS = 4
-FUSE_FROM = 6
+FUSE_FROM = 4
+RING_SHARE = 7 / 32
+LAG = 2
 bf16 = jnp.bfloat16
 f32 = jnp.float32
 
@@ -82,48 +84,86 @@
 
         loop(2, piece)
 
-    def rest(self, run, receive):
+    def handle(self, block, half, up, down, fore, back, run, receive):
+        if receive:
+            self.await_piece(block, half)
+        self.copies(self.view(block, half), block, half, up, down, fore, back, run)
+
+    def pieces(self, distance, body):
+        def one(i):
+            side = 2 * (i // 2) - 1
+            at = self.col + side * distance
+            there = (at >= 0) & (at < SIDE) & (distance >= 0) & ((distance > 0) | (side < 0))
+
+            @pl.when(there)
+            def _():
+                body(side, at, i % 2)
+
+        loop(4, one)
+
+    def turn(self, r, run, receive):
         row, col = self.row, self.col
         yes, no = row >= 0, row < 0
-
-        def pieces(distance, body):
-            def one(i):
-                side = 2 * (i // 2) - 1
-                at = col + side * distance
-                there = (at >= 0) & (at < SIDE) & (distance >= 0) & ((distance > 0) | (side < 0))
-
-                @pl.when(there)
-                def _():
-                    body(side, at, i % 2)
-
-            loop(4, one)
-
-        def handle(block, half, up, down, fore, back):
-            if receive:
-                self.await_piece(block, half)
-            self.copies(self.view(block, half), block, half, up, down, fore, back, run)
 
         def along(side, at, half):
             up = (side < 0) & (col < SIDE - 1)
             down = (side > 0) & (col > 0)
-            handle(row * SIDE + at, half, up, down, yes, yes)
+            self.handle(row * SIDE + at, half, up, down, yes, yes, run, receive)
 
         def around(side, at, half):
-            handle((row + SIDE - 1) % SIDE * SIDE + at, half, no, no, half == 0, no)
-            handle((row + 1) % SIDE * SIDE + at, half, no, no, no, half == 1)
+            self.handle((row + SIDE - 1) % SIDE * SIDE + at, half, no, no, half == 0, no, run, receive)
+            self.handle((row + 1) % SIDE * SIDE + at, half, no, no, no, half == 1, run, receive)
 
         def across(side, at, half):
-            handle((row + 2) % SIDE * SIDE + at, half, no, no, no, no)
-
-        def turn(r):
-            @pl.when(r < SIDE - 1)
-            def _():
-                pieces(r + 1, along)
-
-            pieces(r, around)
-            pieces(r - 1, across)
-
-        loop(SIDE + 1, turn)
+            self.handle((row + 2) % SIDE * SIDE + at, half, no, no, no, no, run, receive)
+
+        @pl.when(r < SIDE - 1)
+        def _():
+            self.pieces(r + 1, along)
+
+        self.pieces(r, around)
+        self.pieces(r - 1, across)
+
+    def rest(self, run, receive):
+        loop(SIDE + 1, lambda r: self.turn(r, run, receive))
+
+
+class RingFirst(Spread):
+    def turn(self, r, run, receive):
+        row, col = self.row, self.col
+        no = row < 0
+        rising, falling = col < SIDE - 1, col > 0
+
+        @pl.when(r == 0)
+        def _():
+            def around(half):
+                before = (row + SIDE - 1) % SIDE * SIDE + col
+                after = (row + 1) % SIDE * SIDE + col
+                self.handle(before, half, rising, falling, half == 0, no, run, receive)
+                self.handle(after, half, rising, falling, no, half == 1, run, receive)
+
+            loop(2, around)
+
+        @pl.when(r == 1)
+        def _():
+            def across(half):
+                self.handle((row + 2) % SIDE * SIDE + col, half, rising, falling, no, no, run, receive)
+
+            loop(2, across)
+
+        @pl.when(r > 1)
+        def _():
+            def along(j):
+                block_row = (row + j + j // 2 * (5 - 2 * j)) % SIDE
+
+                def piece(side, at, half):
+                    up = (side < 0) & rising
+                    down = (side > 0) & falling
+                    self.handle(block_row * SIDE + at, half, up, down, no, no, run, receive)
+
+                self.pieces(r - 1, piece)
+
+            loop(SIDE, along)
 
 
 def start(copy):
@@ -223,14 +263,29 @@
 
     here = (slab, row, col)
 
-    def to_partner(source, block, half):
+    ring = int(width * RING_SHARE) // 32 * 32
+
+    def part(which, half):
+        lowest, size = ((0, ring // 2), (ring, (width - ring) // 2))[which]
+        return pl.ds(pl.multiple_of(lowest + half * size, 16), size)
+
+    def to_partner(which, source, block, half):
         return pltpu.make_async_remote_copy(
             src_ref=source,
-            dst_ref=t_oth.at[half_rows(width, half), block_columns(block)],
-            send_sem=core_send.at[block, half],
-            recv_sem=core_recv.at[block, half],
+            dst_ref=t_oth.at[part(which, half), block_columns(block)],
+            send_sem=core_send.at[which, block, half],
+            recv_sem=core_recv.at[which, block, half],
             device_id=partner,
             device_id_type=MESH,
+        )
+
+    def transfer_part(kind, which, sems):
+        return kind(
+            here,
+            lambda half: transfer_ref.at[part(which, half), :],
+            lambda block, half: t_own.at[part(which, half), block_columns(block)],
+            sems,
+            functools.partial(to_partner, which),
         )
 
     source_spread = Spread(
@@ -239,27 +294,14 @@
         lambda block, half: sources.at[half_rows(rows, half), block_columns(block)],
         spread_sems[0:5],
     )
-    transfer_spread = Spread(
-        here,
-        lambda half: transfer_ref.at[half_rows(width, half), :],
-        lambda block, half: t_own.at[half_rows(width, half), block_columns(block)],
-        spread_sems[5:10],
-        to_partner,
-    )
+    line_first = transfer_part(Spread, 1, spread_sems[5:10])
+    ring_first = transfer_part(RingFirst, 0, spread_sems[15:20])
     contrast_spread = Spread(
         here,
         lambda half: contrast.at[block_rows(trace), half_rows(width, half)],
         lambda block, half: contrast.at[block_rows(block), half_rows(width, half)],
         spread_sems[10:15],
     )
-
-    source_spread.first(start)
-    transfer_spread.first(start)
-    source_spread.rest(start, True)
-    for load in loads:
-        load.wait()
-
-    driven[...] = dot(sources[...], respond[...])
 
     def give_driven(j):
         other, device = peer(j)
@@ -272,25 +314,50 @@
             device_id_type=MESH,
         )
 
-    loop(peers - 1, lambda j: give_driven(j).start())
-    drv_own[:, block_columns(trace)] = driven[block_rows(trace), :]
-
-    transfer_spread.rest(start, True)
-
     def take_driven(j):
         other, _ = peer(j)
         piece = drv_own.at[:, block_columns(other)]
         pltpu.make_async_copy(piece, piece, exchange_recv.at[0, other]).wait()
 
-    loop(peers - 1, take_driven)
     give_d = pltpu.make_async_remote_copy(
         src_ref=drv_own, dst_ref=drv_oth, send_sem=d_send, recv_sem=d_recv, device_id=partner, device_id_type=MESH
     )
-    give_d.start()
+
+    source_spread.first(start)
+    line_first.first(start)
+    ring_first.first(start)
+    turns = SIDE + 1
+    for load in loads:
+        load.wait()
+
+    def gather(i):
+        @pl.when(i < turns)
+        def _():
+            source_spread.turn(i, start, True)
+
+        @pl.when(i == turns)
+        def _():
+            driven[...] = dot(sources[...], respond[...])
+            loop(peers - 1, lambda j: give_driven(j).start())
+            drv_own[:, block_columns(trace)] = driven[block_rows(trace), :]
+
+        @pl.when(i == turns + LAG - 1)
+        def _():
+            loop(peers - 1, take_driven)
+            give_d.start()
+
+        @pl.when(i >= LAG)
+        def _():
+            line_first.turn(i - LAG, start, True)
+            ring_first.turn(i - LAG, start, True)
+
+    loop(turns + LAG, gather)
 
     def take_transfer(i):
-        piece = t_oth.at[half_rows(width, i % 2), block_columns(i // 2)]
-        pltpu.make_async_copy(piece, piece, core_recv.at[i // 2, i % 2]).wait()
+        block, half = i // 2, i % 2
+        for which in range(2):
+            piece = t_oth.at[part(which, half), block_columns(block)]
+            pltpu.make_async_copy(piece, piece, core_recv.at[which, block, half]).wait()
 
     loop(2 * peers, take_transfer)
     give_d.wait()
@@ -321,34 +388,38 @@
         for j in range(CHUNKS):
             emit(j, dot(y_own[...], t_oth[:, columns(j)]) + drv_oth[:, columns(j)])
 
+    def take_rows(operator, store):
+        final = CHUNKS - 1
+        for j in range(final):
+            onward(j).wait_recv()
+            local[...] += dot(x_in[:, columns(j)], operator[columns(j), :])
+        onward(final).wait_recv()
+        for j in range(CHUNKS):
+            store(j, local[:, columns(j)] + dot(x_in[:, columns(final)], operator[columns(final), columns(j)]))
+
+    def keep(j, value):
+        y_own[:, columns(j)] = value.astype(bf16)
+
     @pl.when((place > 0) & (place < FUSE_FROM))
     def _():
-        for j in range(CHUNKS):
-            onward(j).wait_recv()
-        for j in range(CHUNKS):
-            value = dot(x_in[...], t_own[:, columns(j)]) + drv_own[:, columns(j)]
-            y_own[:, columns(j)] = value.astype(bf16)
+        local[...] = drv_own[...]
+        take_rows(t_own, keep)
         for j in range(CHUNKS):
             emit(j, dot(y_own[...], t_oth[:, columns(j)]) + drv_oth[:, columns(j)])
 
     @pl.when(place >= FUSE_FROM)
     def _():
         local[...] = dot(drv_own[...].astype(bf16), t_oth[...]) + drv_oth[...]
-        tall, wide = width // 4, width // 8
+        wide = width // 8
 
         def block(i):
-            at = pl.ds(pl.multiple_of((i % 4) * tall, tall), tall)
-            to = pl.ds(pl.multiple_of((i // 4) * wide, wide), wide)
-            fused[at, to] = dot(t_own[at, :], t_oth[:, to]).astype(bf16)
-
-        loop(32, block)
+            to = pl.ds(pl.multiple_of(i * wide, wide), wide)
+            fused[:, to] = dot(t_own[...], t_oth[:, to]).astype(bf16)
+
+        loop(8, block)
+        take_rows(fused, emit)
         for j in range(CHUNKS):
-            onward(j).wait_recv()
-        for j in range(CHUNKS):
-            emit(j, dot(x_in[...], fused[:, columns(j)]) + local[:, columns(j)])
-        for j in range(CHUNKS):
-            value = dot(x_in[...], t_own[:, columns(j)]) + drv_own[:, columns(j)]
-            y_own[:, columns(j)] = value.astype(bf16)
+            keep(j, dot(x_in[...], t_own[:, columns(j)]) + drv_own[:, columns(j)])
 
     swap = pltpu.make_async_remote_copy(
         src_ref=z_out, dst_ref=z_in, send_sem=z_send, recv_sem=z_recv, device_id=partner, device_id_type=MESH
@@ -392,7 +463,7 @@
 
     loop(peers - 1, lambda j: give_driven(j).wait_send())
     loop(peers - 1, lambda j: give_total(j).wait_send())
-    for spread in (source_spread, transfer_spread, contrast_spread):
+    for spread in (source_spread, line_first, ring_first, contrast_spread):
         spread.first(wait_send)
         spread.rest(wait_send, False)
 
@@ -440,12 +511,12 @@
             dma,
             dma((2, peers)),
             dma((2, peers)),
-            dma((peers, 2)),
-            dma((peers, 2)),
+            dma((2, peers, 2)),
+            dma((2, peers, 2)),
         ]
-        + [dma((peers, 2))] * 15,
+        + [dma((peers, 2))] * 20,
         compiler_params=pltpu.CompilerParams(
-            collective_id=0, has_side_effects=True, vmem_limit_bytes=44 * 2**20
+            collective_id=0, has_side_effects=True, vmem_limit_bytes=60 * 2**20
         ),
         name="sweep",
     )(transfer, respond, reflect, weighted)

time: 207 us -> 201 us (0.971)
  the two profiles are of different devices: /device:TPU:486 before, /device:TPU:24 now
where the time goes in v3:
time: 201 us; the launch traced here: 200 us
  Pallas kernels  197 us (98%)
  local copies, waits for them, and re-layouts  2.24 us (1%)
    pallas_call x1, Pallas kernels, sweep(): pl.pallas_call(functools.partial(sweep_kernel, slabs), out_shape=jax.Shap...  197 us

profile of v3, /device:TPU:24, one launch (start us, length us, event | category | flops | bytes accessed | tf_op | source)
XLA Modules:
  0.0 200.5 jit_solution(14910545607120565814)
XLA Ops:
  0.0 0.0 copy-start
  0.0 0.7 copy-done
  0.7 0.1 mul.11
  0.8 1.6 fusion.weighted_ref
  2.4 196.7 %sweep.1 = bf16[256,128]{1,0:T(8,128)(2,1)} custom-call(bf16[2048,128]{1,0:T(8,128)(2,1)} %bitcast.7, bf16[2048,128]{1,0:T(8,128)(2,1)} %bitcast.8, bf16[2048,128]{1,0:T(8,128)(2,1)} %bitcast.9, bf16[256,128]{1,0:T(8,128)(2,1)} %fusion.weighted_ref), custom_call_target="tpu_custom_call" | custom-call | tf_op jit(solution)/shard_map/sweep/pallas_call | solution.py:482
  199.0 1.5 copy.7
  (1 shorter events, 0.0 us)
Async XLA Ops:
  0.0 0.7 copy-start

commit v4 on v3

--- a/solution.py
+++ b/solution.py
@@ -13,7 +13,6 @@
 SIDE = 4
 CHUNKS = 4
 FUSE_FROM = 4
-RING_SHARE = 7 / 32
 LAG = 2
 bf16 = jnp.bfloat16
 f32 = jnp.float32
@@ -103,19 +102,31 @@
 
     def turn(self, r, run, receive):
         row, col = self.row, self.col
-        yes, no = row >= 0, row < 0
+        no = row < 0
+
+        def handed(at, half):
+            inner = ((col == 1) & (at == 0)) | ((col == SIDE - 2) & (at == SIDE - 1))
+            return inner & (half == 0)
+
+        def lifted(at, half):
+            mine = (at == col) & (half == 0)
+            return mine & (col == 0), mine & (col == SIDE - 1)
 
         def along(side, at, half):
             up = (side < 0) & (col < SIDE - 1)
             down = (side > 0) & (col > 0)
-            self.handle(row * SIDE + at, half, up, down, yes, yes, run, receive)
+            spread = jnp.logical_not(handed(at, half))
+            self.handle(row * SIDE + at, half, up, down, spread, spread, run, receive)
 
         def around(side, at, half):
-            self.handle((row + SIDE - 1) % SIDE * SIDE + at, half, no, no, half == 0, no, run, receive)
-            self.handle((row + 1) % SIDE * SIDE + at, half, no, no, no, half == 1, run, receive)
+            up, down = lifted(at, half)
+            fore = (half == 0) & jnp.logical_not(handed(at, half))
+            self.handle((row + SIDE - 1) % SIDE * SIDE + at, half, up, down, fore, no, run, receive)
+            self.handle((row + 1) % SIDE * SIDE + at, half, up, down, no, half == 1, run, receive)
 
         def across(side, at, half):
-            self.handle((row + 2) % SIDE * SIDE + at, half, no, no, no, no, run, receive)
+            up, down = lifted(at, half)
+            self.handle((row + 2) % SIDE * SIDE + at, half, up, down, no, no, run, receive)
 
         @pl.when(r < SIDE - 1)
         def _():
@@ -126,44 +137,6 @@
 
     def rest(self, run, receive):
         loop(SIDE + 1, lambda r: self.turn(r, run, receive))
-
-
-class RingFirst(Spread):
-    def turn(self, r, run, receive):
-        row, col = self.row, self.col
-        no = row < 0
-        rising, falling = col < SIDE - 1, col > 0
-
-        @pl.when(r == 0)
-        def _():
-            def around(half):
-                before = (row + SIDE - 1) % SIDE * SIDE + col
-                after = (row + 1) % SIDE * SIDE + col
-                self.handle(before, half, rising, falling, half == 0, no, run, receive)
-                self.handle(after, half, rising, falling, no, half == 1, run, receive)
-
-            loop(2, around)
-
-        @pl.when(r == 1)
-        def _():
-            def across(half):
-                self.handle((row + 2) % SIDE * SIDE + col, half, rising, falling, no, no, run, receive)
-
-            loop(2, across)
-
-        @pl.when(r > 1)
-        def _():
-            def along(j):
-                block_row = (row + j + j // 2 * (5 - 2 * j)) % SIDE
-
-                def piece(side, at, half):
-                    up = (side < 0) & rising
-                    down = (side > 0) & falling
-                    self.handle(block_row * SIDE + at, half, up, down, no, no, run, receive)
-
-                self.pieces(r - 1, piece)
-
-            loop(SIDE, along)
 
 
 def start(copy):
@@ -263,29 +236,14 @@
 
     here = (slab, row, col)
 
-    ring = int(width * RING_SHARE) // 32 * 32
-
-    def part(which, half):
-        lowest, size = ((0, ring // 2), (ring, (width - ring) // 2))[which]
-        return pl.ds(pl.multiple_of(lowest + half * size, 16), size)
-
-    def to_partner(which, source, block, half):
+    def to_partner(source, block, half):
         return pltpu.make_async_remote_copy(
             src_ref=source,
-            dst_ref=t_oth.at[part(which, half), block_columns(block)],
-            send_sem=core_send.at[which, block, half],
-            recv_sem=core_recv.at[which, block, half],
+            dst_ref=t_oth.at[half_rows(width, half), block_columns(block)],
+            send_sem=core_send.at[block, half],
+            recv_sem=core_recv.at[block, half],
             device_id=partner,
             device_id_type=MESH,
-        )
-
-    def transfer_part(kind, which, sems):
-        return kind(
-            here,
-            lambda half: transfer_ref.at[part(which, half), :],
-            lambda block, half: t_own.at[part(which, half), block_columns(block)],
-            sems,
-            functools.partial(to_partner, which),
         )
 
     source_spread = Spread(
@@ -294,8 +252,13 @@
         lambda block, half: sources.at[half_rows(rows, half), block_columns(block)],
         spread_sems[0:5],
     )
-    line_first = transfer_part(Spread, 1, spread_sems[5:10])
-    ring_first = transfer_part(RingFirst, 0, spread_sems[15:20])
+    transfer_spread = Spread(
+        here,
+        lambda half: transfer_ref.at[half_rows(width, half), :],
+        lambda block, half: t_own.at[half_rows(width, half), block_columns(block)],
+        spread_sems[5:10],
+        to_partner,
+    )
     contrast_spread = Spread(
         here,
         lambda half: contrast.at[block_rows(trace), half_rows(width, half)],
@@ -324,8 +287,7 @@
     )
 
     source_spread.first(start)
-    line_first.first(start)
-    ring_first.first(start)
+    transfer_spread.first(start)
     turns = SIDE + 1
     for load in loads:
         load.wait()
@@ -348,16 +310,13 @@
 
         @pl.when(i >= LAG)
         def _():
-            line_first.turn(i - LAG, start, True)
-            ring_first.turn(i - LAG, start, True)
+            transfer_spread.turn(i - LAG, start, True)
 
     loop(turns + LAG, gather)
 
     def take_transfer(i):
-        block, half = i // 2, i % 2
-        for which in range(2):
-            piece = t_oth.at[part(which, half), block_columns(block)]
-            pltpu.make_async_copy(piece, piece, core_recv.at[which, block, half]).wait()
+        piece = t_oth.at[half_rows(width, i % 2), block_columns(i // 2)]
+        pltpu.make_async_copy(piece, piece, core_recv.at[i // 2, i % 2]).wait()
 
     loop(2 * peers, take_transfer)
     give_d.wait()
@@ -463,7 +422,7 @@
 
     loop(peers - 1, lambda j: give_driven(j).wait_send())
     loop(peers - 1, lambda j: give_total(j).wait_send())
-    for spread in (source_spread, line_first, ring_first, contrast_spread):
+    for spread in (source_spread, transfer_spread, contrast_spread):
         spread.first(wait_send)
         spread.rest(wait_send, False)
 
@@ -511,10 +470,10 @@
             dma,
             dma((2, peers)),
             dma((2, peers)),
-            dma((2, peers, 2)),
-            dma((2, peers, 2)),
+            dma((peers, 2)),
+            dma((peers, 2)),
         ]
-        + [dma((peers, 2))] * 20,
+        + [dma((peers, 2))] * 15,
         compiler_params=pltpu.CompilerParams(
             collective_id=0, has_side_effects=True, vmem_limit_bytes=60 * 2**20
         ),

time: 201 us -> 193 us (0.960)
  Pallas kernels: 197 us -> 189 us
    pallas_call x1, Pallas kernels: 197 us -> 189 us  [sweep(): pl.pallas_call(functools.partial(sweep_kernel, slabs), out_shape=jax.Shap...]
where the time goes in v4:
time: 193 us
  Pallas kernels  189 us (98%)
  local copies, waits for them, and re-layouts  2.24 us (1%)
    pallas_call x1, Pallas kernels, sweep(): pl.pallas_call(functools.partial(sweep_kernel, slabs), out_shape=jax.Shap...  189 us

profile of v4, /device:TPU:24, one launch (start us, length us, event | category | flops | bytes accessed | tf_op | source)
XLA Modules:
  0.0 192.7 jit_solution(9298975908681527569)
XLA Ops:
  0.0 0.0 copy-start
  0.0 0.7 copy-done
  0.7 0.1 mul.11
  0.8 1.6 fusion.weighted_ref
  2.4 188.9 %sweep.1 = bf16[256,128]{1,0:T(8,128)(2,1)} custom-call(bf16[2048,128]{1,0:T(8,128)(2,1)} %bitcast.7, bf16[2048,128]{1,0:T(8,128)(2,1)} %bitcast.8, bf16[2048,128]{1,0:T(8,128)(2,1)} %bitcast.9, bf16[256,128]{1,0:T(8,128)(2,1)} %fusion.weighted_ref), custom_call_target="tpu_custom_call" | custom-call | tf_op jit(solution)/shard_map/sweep/pallas_call | solution.py:441
  191.2 1.5 copy.7
  (1 shorter events, 0.0 us)
Async XLA Ops:
  0.0 0.7 copy-start

commit v5 on v4

--- a/solution.py
+++ b/solution.py
@@ -67,8 +67,8 @@
         def _():
             send(self.back, (self.slab, (row + SIDE - 1) % SIDE, col))
 
-        if self.extra is not None:
-            run(self.extra(source, block, half))
+        if self.extra is not None and run is start:
+            start(self.extra(source, block, half))
 
     def await_piece(self, block, half):
         piece = self.view(block, half)
@@ -137,6 +137,10 @@
 
     def rest(self, run, receive):
         loop(SIDE + 1, lambda r: self.turn(r, run, receive))
+
+
+def await_bytes(piece, sem):
+    pltpu.make_async_copy(piece, piece, sem).wait()
 
 
 def start(copy):
@@ -192,6 +196,7 @@
     core = slab % 2
     chip = slab // 2
     last = slabs // 2 - 1
+    middle = max(slabs // 4, FUSE_FROM)
     place = chip * (1 - 2 * core) + last * core
     partner = (slab + 1 - 2 * core, row, col)
     following = ((slab + 2 - 4 * core + slabs) % slabs, row, col)
@@ -240,8 +245,8 @@
         return pltpu.make_async_remote_copy(
             src_ref=source,
             dst_ref=t_oth.at[half_rows(width, half), block_columns(block)],
-            send_sem=core_send.at[block, half],
-            recv_sem=core_recv.at[block, half],
+            send_sem=core_send,
+            recv_sem=core_recv,
             device_id=partner,
             device_id_type=MESH,
         )
@@ -271,16 +276,11 @@
         return pltpu.make_async_remote_copy(
             src_ref=driven.at[block_rows(other), :],
             dst_ref=drv_own.at[:, block_columns(trace)],
-            send_sem=exchange_send.at[0, other],
-            recv_sem=exchange_recv.at[0, trace],
+            send_sem=exchange_send.at[0],
+            recv_sem=exchange_recv.at[0],
             device_id=device,
             device_id_type=MESH,
         )
-
-    def take_driven(j):
-        other, _ = peer(j)
-        piece = drv_own.at[:, block_columns(other)]
-        pltpu.make_async_copy(piece, piece, exchange_recv.at[0, other]).wait()
 
     give_d = pltpu.make_async_remote_copy(
         src_ref=drv_own, dst_ref=drv_oth, send_sem=d_send, recv_sem=d_recv, device_id=partner, device_id_type=MESH
@@ -305,7 +305,7 @@
 
         @pl.when(i == turns + LAG - 1)
         def _():
-            loop(peers - 1, take_driven)
+            await_bytes(drv_own.at[:, pl.ds(0, (peers - 1) * depth)], exchange_recv.at[0])
             give_d.start()
 
         @pl.when(i >= LAG)
@@ -314,11 +314,7 @@
 
     loop(turns + LAG, gather)
 
-    def take_transfer(i):
-        piece = t_oth.at[half_rows(width, i % 2), block_columns(i // 2)]
-        pltpu.make_async_copy(piece, piece, core_recv.at[i // 2, i % 2]).wait()
-
-    loop(2 * peers, take_transfer)
+    await_bytes(t_oth, core_recv)
     give_d.wait()
 
     def columns(j):
@@ -341,11 +337,16 @@
         def _():
             onward(j).start()
 
-    @pl.when(place == 0)
-    def _():
-        y_own[...] = drv_own[...].astype(bf16)
-        for j in range(CHUNKS):
-            emit(j, dot(y_own[...], t_oth[:, columns(j)]) + drv_oth[:, columns(j)])
+    swap = pltpu.make_async_remote_copy(
+        src_ref=z_out, dst_ref=z_in, send_sem=z_send, recv_sem=z_recv, device_id=partner, device_id_type=MESH
+    )
+
+    def settle():
+        for spread in (source_spread, transfer_spread):
+            spread.first(wait_send)
+            spread.rest(wait_send, False)
+        await_bytes(t_own, core_send)
+        await_bytes(driven.at[pl.ds(0, (peers - 1) * share), :], exchange_send.at[0])
 
     def take_rows(operator, store):
         final = CHUNKS - 1
@@ -356,6 +357,13 @@
         for j in range(CHUNKS):
             store(j, local[:, columns(j)] + dot(x_in[:, columns(final)], operator[columns(final), columns(j)]))
 
+    @pl.when(place == 0)
+    def _():
+        y_own[...] = drv_own[...].astype(bf16)
+        for j in range(CHUNKS):
+            emit(j, dot(y_own[...], t_oth[:, columns(j)]) + drv_oth[:, columns(j)])
+        swap.start()
+
     def keep(j, value):
         y_own[:, columns(j)] = value.astype(bf16)
 
@@ -365,6 +373,7 @@
         take_rows(t_own, keep)
         for j in range(CHUNKS):
             emit(j, dot(y_own[...], t_oth[:, columns(j)]) + drv_oth[:, columns(j)])
+        swap.start()
 
     @pl.when(place >= FUSE_FROM)
     def _():
@@ -376,14 +385,20 @@
             fused[:, to] = dot(t_own[...], t_oth[:, to]).astype(bf16)
 
         loop(8, block)
+
+        @pl.when(place >= middle)
+        def _():
+            settle()
+
         take_rows(fused, emit)
+        swap.start()
         for j in range(CHUNKS):
             keep(j, dot(x_in[...], t_own[:, columns(j)]) + drv_own[:, columns(j)])
 
-    swap = pltpu.make_async_remote_copy(
-        src_ref=z_out, dst_ref=z_in, send_sem=z_send, recv_sem=z_recv, device_id=partner, device_id_type=MESH
-    )
-    swap.start()
+    @pl.when(place < middle)
+    def _():
+        settle()
+
     swap.wait()
     mine = y_own[...].astype(f32)
     other_way = z_in[...].astype(f32)
@@ -397,8 +412,8 @@
         return pltpu.make_async_remote_copy(
             src_ref=total.at[:, block_columns(other)],
             dst_ref=totals.at[block_rows(trace), :],
-            send_sem=exchange_send.at[1, other],
-            recv_sem=exchange_recv.at[1, trace],
+            send_sem=exchange_send.at[1],
+            recv_sem=exchange_recv.at[1],
             device_id=device,
             device_id_type=MESH,
         )
@@ -407,12 +422,7 @@
     totals[block_rows(trace), :] = total[:, block_columns(trace)]
     contrast_spread.rest(start, True)
 
-    def take_total(j):
-        other, _ = peer(j)
-        piece = totals.at[block_rows(other), :]
-        pltpu.make_async_copy(piece, piece, exchange_recv.at[1, other]).wait()
-
-    loop(peers - 1, take_total)
+    await_bytes(totals.at[pl.ds(0, (peers - 1) * share), :], exchange_recv.at[1])
     out_ref[...] = (totals[...] + dot(contrast[...], reflect[...])).astype(bf16)
 
     @pl.when(place < last)
@@ -420,11 +430,9 @@
         for j in range(CHUNKS):
             onward(j).wait_send()
 
-    loop(peers - 1, lambda j: give_driven(j).wait_send())
-    loop(peers - 1, lambda j: give_total(j).wait_send())
-    for spread in (source_spread, transfer_spread, contrast_spread):
-        spread.first(wait_send)
-        spread.rest(wait_send, False)
+    await_bytes(total.at[:, pl.ds(0, (peers - 1) * depth)], exchange_send.at[1])
+    contrast_spread.first(wait_send)
+    contrast_spread.rest(wait_send, False)
 
 
 def sweep(transfer, respond, reflect, weighted, slabs):
@@ -433,6 +441,7 @@
     peers = SIDE * SIDE
     share = rows // peers
     anywhere = pl.BlockSpec(memory_space=pl.ANY)
+    hbm = pl.BlockSpec(memory_space=pltpu.HBM)
     vmem = pl.BlockSpec(memory_space=pltpu.VMEM)
     dma = pltpu.SemaphoreType.DMA
     operator = pltpu.VMEM((width, width), bf16)
@@ -441,7 +450,7 @@
     return pl.pallas_call(
         functools.partial(sweep_kernel, slabs),
         out_shape=jax.ShapeDtypeStruct((rows, depth), bf16),
-        in_specs=[anywhere] * 4,
+        in_specs=[hbm, hbm, hbm, anywhere],
         out_specs=vmem,
         scratch_shapes=[
             operator,
@@ -468,10 +477,10 @@
             dma((CHUNKS,)),
             dma,
             dma,
-            dma((2, peers)),
-            dma((2, peers)),
-            dma((peers, 2)),
-            dma((peers, 2)),
+            dma((2,)),
+            dma((2,)),
+            dma,
+            dma,
         ]
         + [dma((peers, 2))] * 15,
         compiler_params=pltpu.CompilerParams(

time: 193 us -> 187 us (0.969)
  Pallas kernels: 189 us -> 183 us
    pallas_call x1, Pallas kernels: 189 us -> 183 us  [sweep(): pl.pallas_call(functools.partial(sweep_kernel, slabs), out_shape=jax.Shap...]
where the time goes in v5:
time: 187 us; the launch traced here: 186 us
  Pallas kernels  183 us (98%)
  local copies, waits for them, and re-layouts  2.24 us (1%)
    pallas_call x1, Pallas kernels, sweep(): pl.pallas_call(functools.partial(sweep_kernel, slabs), out_shape=jax.Shap...  183 us

profile of v5, /device:TPU:24, one launch (start us, length us, event | category | flops | bytes accessed | tf_op | source)
XLA Modules:
  0.0 186.4 jit_solution(1687591491527026091)
XLA Ops:
  0.0 0.0 copy-start
  0.0 0.7 copy-done
  0.7 0.1 mul.11
  0.8 1.6 fusion.weighted_ref
  2.4 182.6 %sweep.1 = bf16[256,128]{1,0:T(8,128)(2,1)} custom-call(bf16[2048,128]{1,0:T(8,128)(2,1)} %bitcast.7, bf16[2048,128]{1,0:T(8,128)(2,1)} %bitcast.8, bf16[2048,128]{1,0:T(8,128)(2,1)} %bitcast.9, bf16[256,128]{1,0:T(8,128)(2,1)} %fusion.weighted_ref), custom_call_target="tpu_custom_call" | custom-call | tf_op jit(solution)/shard_map/sweep/pallas_call | solution.py:450
  185.0 1.5 copy.7
  (1 shorter events, 0.0 us)
Async XLA Ops:
  0.0 0.7 copy-start

commit v6 on v5

--- a/solution.py
+++ b/solution.py
@@ -418,9 +418,20 @@
             device_id_type=MESH,
         )
 
-    loop(peers - 1, lambda j: give_total(j).start())
     totals[block_rows(trace), :] = total[:, block_columns(trace)]
-    contrast_spread.rest(start, True)
+
+    def finish(r):
+        contrast_spread.turn(r, start, True)
+
+        @pl.when(r == 0)
+        def _():
+            loop(peers - 1, lambda j: give_total(j).start())
+
+        @pl.when(r >= 2)
+        def _():
+            contrast_spread.turn(r - 2, wait_send, False)
+
+    loop(SIDE + 1, finish)
 
     await_bytes(totals.at[pl.ds(0, (peers - 1) * share), :], exchange_recv.at[1])
     out_ref[...] = (totals[...] + dot(contrast[...], reflect[...])).astype(bf16)
@@ -432,7 +443,7 @@
 
     await_bytes(total.at[:, pl.ds(0, (peers - 1) * depth)], exchange_send.at[1])
     contrast_spread.first(wait_send)
-    contrast_spread.rest(wait_send, False)
+    loop(2, lambda i: contrast_spread.turn(SIDE - 1 + i, wait_send, False))
 
 
 def sweep(transfer, respond, reflect, weighted, slabs):

time: 187 us -> 186 us (level)
  no operation moved by 1% of the time
where the time goes in v6:
time: 186 us; the launch traced here: 185 us
  Pallas kernels  182 us (98%)
  local copies, waits for them, and re-layouts  2.24 us (1%)
    pallas_call x1, Pallas kernels, sweep(): pl.pallas_call(functools.partial(sweep_kernel, slabs), out_shape=jax.Shap...  182 us

profile of v6, /device:TPU:24, one launch (start us, length us, event | category | flops | bytes accessed | tf_op | source)
XLA Modules:
  0.0 185.4 jit_solution(5079209627633741174)
XLA Ops:
  0.0 0.0 copy-start
  0.0 0.7 copy-done
  0.7 0.1 mul.11
  0.8 1.6 fusion.weighted_ref
  2.4 181.5 %sweep.1 = bf16[256,128]{1,0:T(8,128)(2,1)} custom-call(bf16[2048,128]{1,0:T(8,128)(2,1)} %bitcast.7, bf16[2048,128]{1,0:T(8,128)(2,1)} %bitcast.8, bf16[2048,128]{1,0:T(8,128)(2,1)} %bitcast.9, bf16[256,128]{1,0:T(8,128)(2,1)} %fusion.weighted_ref), custom_call_target="tpu_custom_call" | custom-call | tf_op jit(solution)/shard_map/sweep/pallas_call | solution.py:461
  183.9 1.5 copy.7
  (1 shorter events, 0.0 us)
Async XLA Ops:
  0.0 0.7 copy-start
